TPU v7x, 128 devices: a whole 4x4x4 slice. The times are simulated.
128 devices in a mesh: tm: 8 (over y, x_lo), feat: 16 (over x_hi, z, core).
Axes of the slice: x: 4 (x_hi: 2, x_lo: 2; x = x_hi * 2 + x_lo), y: 4, z: 4, core: 2. Of those that a mesh axis runs over, the one named last changes fastest.
Arguments:
- frames: float32 [4096, 8192], P('tm', 'feat'), may hold values from -15 to 25, as said below
Outputs:
- instant: float32 [8192, 8192], P('tm', 'feat')
- lagged: float32 [8192, 8192], P('tm', 'feat')
Inputs may be any that keep to these rules, and one draw needn't show every extreme that they name: `frames`: real-valued feature values.
All inputs are finite; a program needn't handle non-finite values.
Results may differ from a plain program's by a relative error of at most 0.0003.
Values sent between devices are 32-bit elements; how exact they have to be, the bound alone decides.
No kernel may reach another device: no remote copies, remote signals or barrier semaphores. Data moves between devices by JAX's collectives and lax.ppermute only.
A program may use at most 128 MiB of HBM per device.

v0:
```python
import jax
import jax.numpy as jnp
from jax import lax
from jax.sharding import PartitionSpec as P

LAG = 100


def from_behind(block, axis, distance):
    devices = range(lax.axis_size(axis))
    route = [(i - distance, i) for i in devices if i - distance in devices]
    return lax.ppermute(block, axis, route)


def contract_frames(left, right):
    return lax.dot_general(
        left,
        right,
        (((0,), (0,)), ((), ())),
        precision=lax.Precision.HIGHEST,
        preferred_element_type=jnp.float32,
    )


def on_device(frames):
    local_rows = frames.shape[0]
    width = frames.shape[1]
    tm_count = lax.axis_size("tm")
    total = local_rows * tm_count
    sums = lax.psum(jnp.sum(frames, axis=0), "tm")
    centred = frames - sums / total
    ahead = from_behind(centred[:LAG], "tm", -1)
    later = jnp.concatenate([centred[LAG:], ahead], axis=0)
    spread = lax.all_gather(centred, "feat", axis=1, tiled=True)
    paired = jnp.concatenate([centred, later], axis=1)
    owned = lax.psum_scatter(contract_frames(spread, paired), "tm", scatter_dimension=0, tiled=True)
    instant = owned[:, :width] / total
    lagged = owned[:, width:] / (total - LAG)
    return (instant, lagged)


def solution(mesh):
    return jax.shard_map(
        on_device,
        mesh=mesh,
        in_specs=(P("tm", "feat"),),
        out_specs=(P("tm", "feat"), P("tm", "feat")),
        check_vma=False,
    )
```

profile of v0, /device:TPU:1, one launch (start us, length us, event | category | flops | bytes accessed | tf_op | source)
XLA Modules:
  0.0 850.1 jit_solution(5123717104252514771)
XLA Ops:
  7.2 0.0 all-gather.2.cloned.1.call-start
  7.2 1.3 reduce_sum.9
  8.5 17.0 %psum.7 = f32[512]{0:T(512)S(1)} all-reduce(f32[512]{0:T(512)S(1)} %reduce_sum.9), channel_id=1, replica_groups=mesh['tm'=8,'feat'=16] {'tm'}, use_global_device_ids=true, to_apply=%region_1.0 | all-reduce | flops 512 | bytes 4096 | tf_op jit(solution)/shard_map/psum | solution.py:30
  25.6 2.3 broadcast_subtract_fusion
  27.9 0.0 copy-start
  27.9 0.0 all-gather.2.cloned.1.call-update
  27.9 0.0 reduce-scatter.2.cloned.1.call-start
  28.0 1.0 slice.17
  29.0 1.3 collective-permute-start
  30.3 1.2 slice.16
  31.6 4.0 collective-permute-done
  35.6 105.5 %all-gather.2.cloned.1.call-done = f32[512,8192]{1,0:T(8,128)} async-done(((f32[512,512]{1,0:T(8,128)}), f32[512,8192]{1,0:T(8,128)}) %all-gather.2.cloned.1.call-update) | async-done | bytes 16777232 | tf_op jit(solution)/shard_map/all_gather | solution.py:34
  141.1 0.0 copy-done
  141.1 58.9 %fusion = f32[8192,1024]{1,0:T(8,128)} fusion(f32[512,8192]{1,0:T(8,128)} %all-gather.2.cloned.1.call-done, f32[100,512]{1,0:T(8,128)S(1)} %collective-permute-done, f32[412,512]{1,0:T(8,128)S(1)} %slice.16, f32[512,512]{1,0:T(8,128)S(1)} %copy-done), kind=kOutput, calls=%fused_computation.2 | convolution fusion | flops 51540656128 | bytes 52428800 | tf_op jit(solution)/shard_map/dot_general | solution.py:16
  200.1 0.0 reduce-scatter.2.cloned.1.call-update
  200.1 638.4 %reduce-scatter.2.cloned.1.call-done = f32[1024,1024]{1,0:T(8,128)} async-done(((f32[8192,1024]{1,0:T(8,128)}), f32[1024,1024]{1,0:T(8,128)}) %reduce-scatter.2.cloned.1.call-update) | async-done | bytes 4194320 | tf_op jit(solution)/shard_map/reduce_scatter | solution.py:36
  838.5 4.7 slice_multiply_fusion
  (1 shorter events, 0.0 us)
Async XLA Ops:
  7.2 134.0 %all-gather.2.cloned.1.call-start = ((), (), s32[]{:S(2)}) async-start(), calls=%async_computation.1 | async-start | bytes 17825792 | tf_op jit(solution)/shard_map/all_gather | solution.py:34
  27.9 113.2 %copy-start = (f32[512,512]{1,0:T(8,128)S(1)}, f32[512,512]{1,0:T(8,128)}, u32[]{:S(2)}) copy-start(f32[512,512]{1,0:T(8,128)} %broadcast_subtract_fusion) | copy-start | bytes 3145732
  27.9 810.6 %reduce-scatter.2.cloned.1.call-start = ((), (), s32[]{:S(2)}) async-start(), calls=%async_computation.2 | async-start | bytes 37748736 | tf_op jit(solution)/shard_map/reduce_scatter | solution.py:36
  29.0 6.6 collective-permute-start
Sparse Core Ops, SparseCore 0:
  28.1 113.0 all-gather.1
  200.2 638.2 reduce-scatter.1
where the time goes:
time: 850 us
  waiting for transfers between devices  748 us (88%)
  matrix products  58.9 us (7%)
  blocking collectives  17 us (2%)
  between operations  14.1 us (2%)
    reduce_scatter x1, waiting for transfers between devices, on_device(): lax.psum_scatter(contract_frames(spread, paired), 'tm', scatter_dimension...  638 us
    all_gather x1, waiting for transfers between devices, on_device(): spread = lax.all_gather(centred, 'feat', axis=1, tiled=True)  106 us
    dot_general x1, matrix products, contract_frames(): lax.dot_general(left, right, (((0,), (0,)), ((), ())), precision=lax.Prec...  58.9 us
    psum x1, blocking collectives, on_device(): sums = lax.psum(jnp.sum(frames, axis=0), 'tm')  17 us
  transfers between devices with their start and end apart: 3, of which 3 were waited for; matrix products, arithmetic and copies ran while one was open for 0% of the time, Pallas kernels for 0%

commit v1 on v0

v1 whole, which is shorter than its diff:
```python
import functools

import jax
import jax.numpy as jnp
from jax import lax
from jax.experimental import pallas as pl
from jax.experimental.pallas import tpu as pltpu
from jax.sharding import PartitionSpec as P

LAG = 100
AXES = ("tm", "feat")
DEVICES = 128
SLOTS = 8
VMEM = 40 * 2**20


def place(device):
    tm, feat = divmod(device, 16)
    return feat // 8, tm % 2, tm // 2, feat // 2 % 4, feat % 2


def device_at(x_hi, x_lo, y, z, core):
    return (y % 4 * 2 + x_lo) * 16 + (x_hi * 4 + z % 4) * 2 + core


def move(block, step):
    route = [(d, device_at(*step(*place(d)))) for d in range(DEVICES)]
    return lax.ppermute(block, AXES, route)


def along_x_lo(block):
    return move(block, lambda xh, xl, y, z, c: (xh, 1 - xl, y, z, c))


def along_x_hi(block):
    return move(block, lambda xh, xl, y, z, c: (1 - xh, xl, y, z, c))


def along_y(block, n):
    return move(block, lambda xh, xl, y, z, c: (xh, xl, y + n, z, c))


def along_z(block, n):
    return move(block, lambda xh, xl, y, z, c: (xh, xl, y, z + n, c))


def other_core(block):
    return move(block, lambda xh, xl, y, z, c: (xh, xl, y, z, 1 - c))


def pair_in_plane(turn, y):
    return 2 * (turn // 2 ^ y // 2) + (turn % 2 ^ y % 2)


def to_row_owner(block, turn):
    def step(xh, xl, y, z, c):
        pair = pair_in_plane(turn, y)
        return xh ^ pair // 2 ^ xl, pair % 2, 2 * xh + pair // 2, z, c

    return move(block, step)


together = lax.optimization_barrier


def split(x):
    high = x.astype(jnp.bfloat16)
    return high, (x - high.astype(jnp.float32)).astype(jnp.bfloat16)


def columns_kernel(sizes, first, rows_ref, *refs):
    n = len(sizes)
    pieces, refs = refs[:n], refs[n:]
    if first:
        high_out, low_out, centre_out, sums_out, high, low, sems = refs
        block = pieces[0][...]
        centre = jnp.sum(block, axis=0, keepdims=True) / block.shape[0]
        centre_out[...] = centre
        sums = jnp.zeros_like(centre)
    else:
        centre_in, sums_in, _, _, high_out, low_out, sums_out, high, low, sems = refs
        centre, sums = centre_in[...], sums_in[...]
    copies, at = [], 0
    for i, size in enumerate(sizes):
        block = pieces[i][...] - centre
        sums = sums + jnp.sum(block, axis=0, keepdims=True)
        here = pl.ds(at, size)
        high[here, :], low[here, :] = split(block)
        there = pl.ds(pl.multiple_of(rows_ref[i], 128), size)
        for j, (held, out) in enumerate(((high, high_out), (low, low_out))):
            copy = pltpu.make_async_copy(held.at[here], out.at[there], sems.at[2 * i + j])
            copy.start()
            copies.append(copy)
        at += size
    sums_out[...] = sums
    for copy in copies:
        copy.wait()


def split_columns(pieces, starts, total, state=None):
    sizes = [p.shape[0] for p in pieces]
    width = pieces[0].shape[1]
    n, first = len(pieces), state is None
    whole = jax.ShapeDtypeStruct((total, width), jnp.bfloat16)
    line = jax.ShapeDtypeStruct((1, width), jnp.float32)
    anywhere = pl.BlockSpec(memory_space=pl.ANY)
    held = pl.BlockSpec(memory_space=pltpu.VMEM)
    more, more_specs, aliases = [], [], {}
    if not first:
        high, low, centre, sums = state
        more, more_specs = [centre, sums, high, low], [held, held, anywhere, anywhere]
        aliases = {n + 3: 0, n + 4: 1}
    count = sum(sizes) * width
    out = pl.pallas_call(
        functools.partial(columns_kernel, sizes, first),
        grid_spec=pltpu.PrefetchScalarGridSpec(
            num_scalar_prefetch=1,
            grid=(),
            in_specs=[held] * n + more_specs,
            out_specs=[anywhere, anywhere] + [held] * (2 if first else 1),
            scratch_shapes=[
                pltpu.VMEM((sum(sizes), width), jnp.bfloat16),
                pltpu.VMEM((sum(sizes), width), jnp.bfloat16),
                pltpu.SemaphoreType.DMA((2 * n,)),
            ],
        ),
        out_shape=[whole, whole] + [line] * (2 if first else 1),
        input_output_aliases=aliases,
        cost_estimate=pl.CostEstimate(flops=6 * count, bytes_accessed=8 * count, transcendentals=0),
        compiler_params=pltpu.CompilerParams(vmem_limit_bytes=VMEM),
        name="split_columns",
    )(jnp.stack(starts).astype(jnp.int32), *pieces, *more)
    if first:
        return out
    return out[0], out[1], state[2], out[2]


def rows_kernel(facts_ref, *refs):
    pieces, (high_out, low_out, edge_out, held) = refs[:4], refs[4:]
    step = pl.program_id(0)
    count, rows, frames = pieces[0].shape

    @pl.when(step == 0)
    def _():
        for half in range(2):
            near, late = pieces[2 * half], pieces[2 * half + 1]
            total = jnp.zeros((rows, frames), jnp.float32)
            for i in range(count):
                total = total + (near[i] + late[i])
            mean = jnp.sum(total, axis=1, keepdims=True) / (2 * count * frames)
            core = facts_ref[0] if half == 0 else 1 - facts_ref[0]
            there = pl.ds(pl.multiple_of(core * rows, rows), rows)
            for i in range(count):
                held[i, there, :] = near[i] - mean
                held[count + i, there, :] = late[i] - mean
        edge_out[...] = jnp.zeros_like(edge_out)

    now = held[step]
    before = held[facts_ref[1 + step]]
    before = jnp.where(facts_ref[1 + SLOTS + step] == 0, 0.0, before)
    lane = lax.broadcasted_iota(jnp.int32, now.shape, 1)
    shifted = jnp.where(lane < LAG, pltpu.roll(before, LAG, 1), pltpu.roll(now, LAG, 1))
    edge_out[...] += jnp.sum(shifted, axis=1, keepdims=True)
    high_out[0, : 2 * rows], low_out[0, : 2 * rows] = split(now)
    high_out[0, 2 * rows :], low_out[0, 2 * rows :] = split(shifted)


def split_rows(near, late, near_other, late_other, facts):
    count, rows, frames = near.shape
    whole = jax.ShapeDtypeStruct((SLOTS, 4 * rows, frames), jnp.bfloat16)
    once = pl.BlockSpec((count, rows, frames), lambda s, f: (0, 0, 0), pipeline_mode=pl.Buffered(1))
    each = pl.BlockSpec((1, 4 * rows, frames), lambda s, f: (s, 0, 0))
    size = SLOTS * 2 * rows * frames
    return pl.pallas_call(
        rows_kernel,
        grid_spec=pltpu.PrefetchScalarGridSpec(
            num_scalar_prefetch=1,
            grid=(SLOTS,),
            in_specs=[once] * 4,
            out_specs=[each, each, pl.BlockSpec((2 * rows, 128), lambda s, f: (0, 0))],
            scratch_shapes=[pltpu.VMEM((SLOTS, 2 * rows, frames), jnp.float32)],
        ),
        out_shape=[whole, whole, jax.ShapeDtypeStruct((2 * rows, 128), jnp.float32)],
        cost_estimate=pl.CostEstimate(flops=10 * size, bytes_accessed=12 * size, transcendentals=0),
        compiler_params=pltpu.CompilerParams(vmem_limit_bytes=VMEM),
        name="split_rows",
    )(facts, near, late, near_other, late_other)


def product_kernel(first, facts_ref, ah, al, edge, bh, bl, sums, *refs):
    instant_out, lagged_out, total = refs if first else refs[2:]
    step = pl.program_id(0)
    dot = functools.partial(jnp.dot, preferred_element_type=jnp.float32)
    high, low, right = ah[0], al[0], bh[0]
    part = dot(high, right) + dot(low, right) + dot(high, bl[0])

    @pl.when(step == 0)
    def _():
        total[...] = part

    @pl.when((step > 0) & (step < SLOTS - 1))
    def _():
        total[...] += part

    @pl.when(step == SLOTS - 1)
    def _():
        done = total[...] + part
        rows = done.shape[0] // 2
        frames = SLOTS * high.shape[1]
        off = sums[...] / frames
        instant_out[...] = (done[:rows] / frames).reshape(instant_out.shape)
        lagged = (done[rows:] - edge[:, :1] * off) / (frames - LAG)
        lagged_out[...] = lagged.reshape(lagged_out.shape)


def product(rows, columns, facts, outs):
    ah, al, edge = rows
    bh, bl, _, sums = columns
    _, m, frames = ah.shape
    width = bh.shape[1]
    quarter = m // 4
    bh, bl = (b.reshape(SLOTS, frames, width) for b in (bh, bl))
    left = pl.BlockSpec((1, m, frames), lambda s, f: (s, 0, 0))
    right = pl.BlockSpec((1, frames, width), lambda s, f: (f[1 + s], 0, 0))
    out = pl.BlockSpec((2, 1, quarter, width), lambda s, f: (0, f[0], 0, 0))
    shape = jax.ShapeDtypeStruct((2, 4, quarter, width), jnp.float32)
    first = outs is None
    more = () if first else outs
    flops = 2 * 3 * SLOTS * m * frames * width
    return pl.pallas_call(
        functools.partial(product_kernel, first),
        grid_spec=pltpu.PrefetchScalarGridSpec(
            num_scalar_prefetch=1,
            grid=(SLOTS,),
            in_specs=[
                left,
                left,
                pl.BlockSpec((2 * quarter, 128), lambda s, f: (0, 0)),
                right,
                right,
                pl.BlockSpec((1, width), lambda s, f: (0, 0)),
            ]
            + [pl.BlockSpec(memory_space=pl.ANY)] * len(more),
            out_specs=[out, out],
            scratch_shapes=[pltpu.VMEM((m, width), jnp.float32)],
        ),
        out_shape=[shape, shape],
        input_output_aliases={} if first else {7: 0, 8: 1},
        cost_estimate=pl.CostEstimate(
            flops=flops, bytes_accessed=4 * SLOTS * frames * (m + width), transcendentals=0
        ),
        compiler_params=pltpu.CompilerParams(vmem_limit_bytes=VMEM),
        name="product",
    )(facts, ah, al, edge, bh, bl, sums, *more)


def on_device(frames):
    rows, width = frames.shape
    half, fourth = rows // 2, rows // 4
    quarter = width // 4
    total = SLOTS * rows
    tm, feat = lax.axis_index("tm"), lax.axis_index("feat")
    y, x_lo, x_hi, z, core = tm // 2, tm % 2, feat // 8, feat // 2 % 4, feat % 2

    own = frames
    quarters = own.T.reshape(4, quarter, rows)
    spread = [quarters[0]] + [along_z(quarters[n], n) for n in (1, 2, 3)]
    below1, above1 = along_y(own[:half], 1), along_y(own[:half], -1)
    other1 = along_x_lo(own[:half])
    *spread, below1, above1, other1 = together((*spread, below1, above1, other1))

    spread = jnp.stack(spread)
    landed = []
    for turn in range(4):
        which = lax.rem(z - pair_in_plane(turn, y) + 4, 4)
        landed.append(to_row_owner(lax.dynamic_index_in_dim(spread, which, 0, keepdims=False), turn))
    *landed, own = together((*landed, own))

    swapped = [along_x_hi(landed[0]), along_x_hi(landed[1])]
    below2, above2 = along_y(own[half:], 1), along_y(own[half:], -1)
    *swapped, below2, above2, own, late1, late2, other1 = together((*swapped, below2, above2, own, *landed[2:], other1))

    near = jnp.stack([landed[0], swapped[0], landed[1], swapped[1]])
    swapped = [along_x_hi(late1), along_x_hi(late2)]
    other2 = along_x_lo(own[half:])
    below_near, above_near = along_z(near, 1), along_z(near, -1)
    far1, far2 = along_y(below1, 1), along_y(above2, -1)
    cross_below1, cross_above1 = along_y(other1, 1), along_y(other1, -1)
    *swapped, other2, near, below_near, above_near, far1, far2, cross_below1, cross_above1 = together(
        (*swapped, other2, near, below_near, above_near, far1, far2, cross_below1, cross_above1)
    )

    late = jnp.stack([late1, swapped[0], late2, swapped[1]])
    below_late, above_late = along_z(late, 1), along_z(late, -1)
    cross_below2, cross_above2 = along_y(other2, 1), along_y(other2, -1)
    cross_far1, cross_far2 = along_y(cross_below1[:fourth], 1), along_y(cross_above1[fourth:], -1)
    near_other, below_near_other, above_near_other = (other_core(b) for b in (near, below_near, above_near))
    late, below_late, above_late, below_near, above_near, cross_below2, cross_above2, cross_far1, cross_far2 = together(
        (late, below_late, above_late, below_near, above_near, cross_below2, cross_above2, cross_far1, cross_far2)
    )

    far_near, far_late = along_z(below_near, 1), along_z(above_late, -1)
    cross_far3, cross_far4 = along_y(cross_below2[:fourth], 1), along_y(cross_above2[fourth:], -1)
    late_other, below_late_other, above_late_other = (other_core(b) for b in (late, below_late, above_late))
    far_near_other, far_late_other = other_core(far_near), other_core(far_late)

    def start(y_off, x_from, skip):
        return (lax.rem(y + y_off + 4, 4) * 2 + x_from) * rows + skip

    here, cross = x_lo, 1 - x_lo
    columns = split_columns(
        [own, other1, other2, below1, below2, above1, above2, far1, far2, cross_below1, cross_above1, cross_far1, cross_far2],
        [
            start(0, here, 0),
            start(0, cross, 0),
            start(0, cross, half),
            start(-1, here, 0),
            start(-1, here, half),
            start(1, here, 0),
            start(1, here, half),
            start(-2, here, 0),
            start(2, here, half),
            start(-1, cross, 0),
            start(1, cross, 0),
            start(-2, cross, 0),
            start(2, cross, fourth),
        ],
        total,
    )
    columns = split_columns(
        [cross_below2, cross_above2, cross_far3, cross_far4],
        [start(-1, cross, half), start(1, cross, half), start(-2, cross, half), start(2, cross, half + fourth)],
        total,
        columns,
    )

    times = []
    x_first = x_hi ^ y // 2 ^ y % 2
    for turn in range(4):
        y_from = 2 * (y % 2 ^ turn // 2) + (x_lo ^ turn % 2)
        times += [2 * y_from + x_first, 2 * y_from + 1 - x_first]
    times = jnp.stack(times).astype(jnp.int32)
    before = jnp.argmax(times[None, :] == jnp.maximum(times - 1, 0)[:, None], axis=1).astype(jnp.int32)
    row_facts = jnp.concatenate([core.astype(jnp.int32)[None], before, times])
    first = z - (y % 2 * 2 + x_lo)

    def facts(away):
        return jnp.concatenate([lax.rem(first + away + 8, 4).astype(jnp.int32)[None], times])

    outs = None
    for away, parts in (
        (0, (near, late, near_other, late_other)),
        (-1, (below_near, below_late, below_near_other, below_late_other)),
        (1, (above_near, above_late, above_near_other, above_late_other)),
        (2, (far_near, far_late, far_near_other, far_late_other)),
    ):
        outs = product(split_rows(*parts, row_facts), columns, facts(away), outs)
    return tuple(out.reshape(2 * width, width) for out in outs)


def solution(mesh):
    return jax.shard_map(
        on_device,
        mesh=mesh,
        in_specs=(P("tm", "feat"),),
        out_specs=(P("tm", "feat"), P("tm", "feat")),
        check_vma=False,
    )
```

time: 850 us -> 275 us (0.32)
  waiting for transfers between devices: 748 us -> 72.2 us
  Pallas kernels: 0 us -> 77.4 us
  starting transfers between devices: 1.37 us -> 68.2 us
  matrix products: 58.9 us -> 0 us
  local copies, waits for them, and re-layouts: 2.28 us -> 49.7 us
  blocking collectives: 17 us -> 0 us
  between operations: 14.1 us -> 1.13 us
    reduce_scatter x1 -> x0, waiting for transfers between devices: 638 us -> none  [on_device(): lax.psum_scatter(contract_frames(spread, paired), 'tm', scatter_dimension...]
    all_gather x1 -> x0, waiting for transfers between devices: 106 us -> none  [on_device(): spread = lax.all_gather(centred, 'feat', axis=1, tiled=True)]
    pallas_call x0 -> x10, Pallas kernels: none -> 77.4 us  [the longest x4 46 us: product(): pl.pallas_call(functools.partial(product_kernel, first), grid_spec=pltpu....]
    ppermute x1 -> x41, waiting for transfers between devices: 4.03 us -> 72.2 us  [move(): return lax.ppermute(block, AXES, route)]
    ppermute x1 -> x41, starting transfers between devices: 1.29 us -> 68.2 us  [move(): return lax.ppermute(block, AXES, route)]
    dot_general x1 -> x0, matrix products: 58.9 us -> none  [contract_frames(): lax.dot_general(left, right, (((0,), (0,)), ((), ())), precision=lax.Prec...]
    unnamed x2 -> x94, local copies, waits for them, and re-layouts: 0.01 us -> 40.8 us
    psum x1 -> x0, blocking collectives: 17 us -> none  [on_device(): sums = lax.psum(jnp.sum(frames, axis=0), 'tm')]
  transfers between devices with their start and end apart: 3 -> 41, of which waited for: 3 -> 15; matrix products, arithmetic and copies ran while one was open for 0% -> 2% of each run, Pallas kernels for 0% -> 22%
where the time goes in v1:
time: 275 us; the launch traced here: 273 us
  Pallas kernels  77.4 us (28%)
  waiting for transfers between devices  72.2 us (26%)
  starting transfers between devices  68.2 us (25%)
  local copies, waits for them, and re-layouts  49.7 us (18%)
  other arithmetic  4.47 us (2%)
    ppermute x41, waiting for transfers between devices, move(): return lax.ppermute(block, AXES, route)  72.2 us
    ppermute x41, starting transfers between devices, move(): return lax.ppermute(block, AXES, route)  68.2 us
    pallas_call x4, Pallas kernels, product(): pl.pallas_call(functools.partial(product_kernel, first), grid_spec=pltpu....  46 us
    unnamed x94, local copies, waits for them, and re-layouts  40.8 us
    pallas_call x4, Pallas kernels, split_rows(): pl.pallas_call(rows_kernel, grid_spec=pltpu.PrefetchScalarGridSpec(num_sc...  25.2 us
    pallas_call x2, Pallas kernels, split_columns(): pl.pallas_call(functools.partial(columns_kernel, sizes, first), grid_spec...  6.21 us
  transfers between devices with their start and end apart: 41, of which 15 were waited for; matrix products, arithmetic and copies ran while one was open for 2% of the time, Pallas kernels for 22%

profile of v1, /device:TPU:1, one launch (start us, length us, event | category | flops | bytes accessed | tf_op | source)
XLA Modules:
  0.0 273.2 jit_solution(18311551486630429506)
XLA Ops:
  0.6 2.0 fusion
  2.6 2.5 collective-permute-start
  5.1 1.9 slice.44
  7.0 1.3 collective-permute-start.3
  8.2 1.4 collective-permute-start.4
  9.7 1.2 collective-permute-start.5
  10.9 3.3 %collective-permute-start.1 = (f32[128,512]{0,1:T(8,128)}, f32[128,512]{0,1:T(8,128)}, u32[]{:S(2)}, u32[]{:S(2)}) collective-permute-start(f32[128,512]{0,1:T(8,128)} %get-tuple-element.141), channel_id=1, source_target_pairs={{0,4},{1,5},{2,6},{3,7},{4,0},{5,1},{6,2},{7,3},{8,12},{9,13},{10,... | collective-permute-start | bytes 786440 | tf_op jit(solution)/shard_map/ppermute | solution.py:28
  14.9 4.5 %collective-permute-done.1 = f32[128,512]{0,1:T(8,128)} collective-permute-done((f32[128,512]{0,1:T(8,128)}, f32[128,512]{0,1:T(8,128)}, u32[]{:S(2)}, u32[]{:S(2)}) %collective-permute-start.1) | collective-permute-done | bytes 262176 | tf_op jit(solution)/shard_map/ppermute | solution.py:28
  19.4 5.9 %collective-permute-done.2 = f32[128,512]{0,1:T(8,128)} collective-permute-done((f32[128,512]{0,1:T(8,128)S(1)}, f32[128,512]{0,1:T(8,128)}, u32[]{:S(2)}, u32[]{:S(2)}) %collective-permute-start.2) | collective-permute-done | bytes 262176 | tf_op jit(solution)/shard_map/ppermute | solution.py:28
  25.3 1.5 pad_maximum_fusion
  27.6 1.8 copy.15
  29.3 3.6 %collective-permute-start.6 = (f32[128,512]{1,0:T(8,128)}, f32[128,512]{1,0:T(8,128)}, u32[]{:S(2)}, u32[]{:S(2)}) collective-permute-start(f32[128,512]{1,0:T(8,128)} %bitcast.61), channel_id=1, source_target_pairs={{0,0},{1,1},{2,2},{3,3},{4,4},{5,5},{6,6},{7,7},{8,72},{9,73},{10,... | collective-permute-start | bytes 786440 | tf_op jit(solution)/shard_map/ppermute | solution.py:28
  34.4 3.9 %collective-permute-start.8 = (f32[128,512]{1,0:T(8,128)S(1)}, f32[128,512]{1,0:T(8,128)}, u32[]{:S(2)}, u32[]{:S(2)}) collective-permute-start(f32[128,512]{1,0:T(8,128)S(1)} %bitcast.63), channel_id=1, source_target_pairs={{0,40},{1,41},{2,42},{3,43},{4,44},{5,45},{6,46},{7,47},{8,96},{9,... | collective-permute-start | bytes 786440 | tf_op jit(solution)/shard_map/ppermute | solution.py:28
  40.2 7.9 %collective-permute-done.8 = f32[128,512]{1,0:T(8,128)} collective-permute-done((f32[128,512]{1,0:T(8,128)S(1)}, f32[128,512]{1,0:T(8,128)}, u32[]{:S(2)}, u32[]{:S(2)}) %collective-permute-start.8) | collective-permute-done | bytes 262176 | tf_op jit(solution)/shard_map/ppermute | solution.py:28
  48.1 4.9 %collective-permute-done.9 = f32[128,512]{1,0:T(8,128)S(1)} collective-permute-done((f32[128,512]{1,0:T(8,128)S(1)}, f32[128,512]{1,0:T(8,128)S(1)}, u32[]{:S(2)}, u32[]{:S(2)}) %collective-permute-start.9) | collective-permute-done | bytes 262176 | tf_op jit(solution)/shard_map/ppermute | solution.py:28
  53.0 2.7 collective-permute-start.13
  56.7 1.9 collective-permute-start.11
  58.7 4.0 %collective-permute-done.10 = f32[128,512]{1,0:T(8,128)S(1)} collective-permute-done((f32[128,512]{1,0:T(8,128)}, f32[128,512]{1,0:T(8,128)S(1)}, u32[]{:S(2)}, u32[]{:S(2)}) %collective-permute-start.10) | collective-permute-done | bytes 262176 | tf_op jit(solution)/shard_map/ppermute | solution.py:28
  62.7 5.2 %collective-permute-done.11 = f32[128,512]{1,0:T(8,128)S(1)} collective-permute-done((f32[128,512]{1,0:T(8,128)}, f32[128,512]{1,0:T(8,128)S(1)}, u32[]{:S(2)}, u32[]{:S(2)}) %collective-permute-start.11) | collective-permute-done | bytes 262176 | tf_op jit(solution)/shard_map/ppermute | solution.py:28
  68.6 1.1 pad_maximum_fusion.1.refs_0_
  69.7 4.2 %collective-permute-start.17 = (f32[4,128,512]{2,1,0:T(8,128)S(1)}, f32[4,128,512]{2,1,0:T(8,128)}, u32[]{:S(2)}, u32[]{:S(2)}) collective-permute-start(f32[4,128,512]{2,1,0:T(8,128)S(1)} %pad_maximum_fusion.1.refs_0_), channel_id=1, source_target_pairs={{0,2},{1,3},{2,4},{3,5},{4,6},{5,7},{6,0},{7,1},{8,10},{9,11},{10,... | collective-permute-start | bytes 3145736 | tf_op jit(solution)/shard_map/ppermute | solution.py:28
  73.9 2.1 collective-permute-start.14
  78.2 5.4 %collective-permute-done.14 = f32[128,512]{1,0:T(8,128)S(1)} collective-permute-done((f32[128,512]{1,0:T(8,128)}, f32[128,512]{1,0:T(8,128)S(1)}, u32[]{:S(2)}, u32[]{:S(2)}) %collective-permute-start.14) | collective-permute-done | bytes 262176 | tf_op jit(solution)/shard_map/ppermute | solution.py:28
  83.7 1.1 collective-permute-start.20
  84.8 4.8 %collective-permute-done.15 = f32[128,512]{1,0:T(8,128)S(1)} collective-permute-done((f32[128,512]{1,0:T(8,128)S(1)}, f32[128,512]{1,0:T(8,128)S(1)}, u32[]{:S(2)}, u32[]{:S(2)}) %collective-permute-start.15) | collective-permute-done | bytes 262176 | tf_op jit(solution)/shard_map/ppermute | solution.py:28
  89.7 2.5 collective-permute-start.22
  93.1 6.5 %collective-permute-done.21.refs_9_ = f32[256,512]{1,0:T(8,128)S(1)} collective-permute-done((f32[256,512]{1,0:T(8,128)S(1)}, f32[256,512]{1,0:T(8,128)S(1)}, u32[]{:S(2)}, u32[]{:S(2)}) %collective-permute-start.21) | collective-permute-done | bytes 524320 | tf_op jit(solution)/shard_map/ppermute | solution.py:28
  99.6 5.0 %collective-permute-done.22.refs_10_ = f32[256,512]{1,0:T(8,128)S(1)} collective-permute-done((f32[256,512]{1,0:T(8,128)S(1)}, f32[256,512]{1,0:T(8,128)S(1)}, u32[]{:S(2)}, u32[]{:S(2)}) %collective-permute-start.22) | collective-permute-done | bytes 524320 | tf_op jit(solution)/shard_map/ppermute | solution.py:28
  104.6 1.1 copy-done.11
  106.7 4.5 %collective-permute-start.23 = (f32[4,128,512]{2,1,0:T(8,128)S(1)}, f32[4,128,512]{2,1,0:T(8,128)}, u32[]{:S(2)}, u32[]{:S(2)}) collective-permute-start(f32[4,128,512]{2,1,0:T(8,128)S(1)} %pad_maximum_fusion.2.refs_1_), channel_id=1, source_target_pairs={{0,2},{1,3},{2,4},{3,5},{4,6},{5,7},{6,0},{7,1},{8,10},{9,11},{10,... | collective-permute-start | bytes 3145736 | tf_op jit(solution)/shard_map/ppermute | solution.py:28
  111.2 2.1 collective-permute-start.25
  113.5 2.7 collective-permute-start.28
  116.2 8.5 %collective-permute-done.27.refs_11_ = f32[128,512]{1,0:T(8,128)S(1)} collective-permute-done((f32[128,512]{1,0:T(8,128)S(1)}, f32[128,512]{1,0:T(8,128)S(1)}, u32[]{:S(2)}, u32[]{:S(2)}) %collective-permute-start.27) | collective-permute-done | bytes 262176 | tf_op jit(solution)/shard_map/ppermute | solution.py:28
  126.8 7.9 %collective-permute-start.39 = (f32[4,128,512]{2,1,0:T(8,128)S(1)}, f32[4,128,512]{2,1,0:T(8,128)S(1)}, u32[]{:S(2)}, u32[]{:S(2)}) collective-permute-start(f32[4,128,512]{2,1,0:T(8,128)S(1)} %pad_maximum_fusion.1.refs_0_), channel_id=1, source_target_pairs={{0,1},{1,0},{2,3},{3,2},{4,5},{5,4},{6,7},{7,6},{8,9},{9,8},{10,11... | collective-permute-start | bytes 3145736 | tf_op jit(solution)/shard_map/ppermute | solution.py:28
  134.7 6.9 %collective-permute-start.40 = (f32[4,128,512]{2,1,0:T(8,128)S(1)}, f32[4,128,512]{2,1,0:T(8,128)}, u32[]{:S(2)}, u32[]{:S(2)}) collective-permute-start(f32[4,128,512]{2,1,0:T(8,128)S(1)} %pad_maximum_fusion.2.refs_1_), channel_id=1, source_target_pairs={{0,1},{1,0},{2,3},{3,2},{4,5},{5,4},{6,7},{7,6},{8,9},{9,8},{10,11... | collective-permute-start | bytes 3145736 | tf_op jit(solution)/shard_map/ppermute | solution.py:28
  141.6 1.1 collective-permute-start.33
  142.7 1.5 collective-permute-start.29
  145.2 1.2 collective-permute-start.30
  149.7 1.4 collective-permute-done.33.refs_2_
  152.4 6.9 %collective-permute-done.34.refs_3_ = f32[128,512]{1,0:T(8,128)} collective-permute-done((f32[128,512]{1,0:T(8,128)}, f32[128,512]{1,0:T(8,128)}, u32[]{:S(2)}, u32[]{:S(2)}) %collective-permute-start.34) | collective-permute-done | bytes 262176 | tf_op jit(solution)/shard_map/ppermute | solution.py:28
  159.3 1.6 collective-permute-start.35
  162.4 1.1 copy-done.8
  163.5 1.0 copy-done.10
  165.6 1.0 copy-done.20
  173.8 3.6 %split_columns.2 = (bf16[4096,512]{1,0:T(8,128)(2,1)S(1)}, bf16[4096,512]{1,0:T(8,128)(2,1)}, f32[1,512]{1,0:T(1,128)S(1)}, f32[1,512]{1,0:T(1,128)S(1)}) custom-call(s32[13]{0:T(128)S(1)} %stack.171.rows_ref, f32[512,512]{1,0:T(8,128)S(1)} %copy-done, f32[256,512]{1,0:T(8,128)S(1)} %copy-done.22, f32[256,512]{1,0:T(8,128)S(1)} %copy-done.30, ...), custom_call_target="tpu_custom_call" | custom-call | flops 10223616 | bytes 13631488 | tf_op jit(solution)/shard_map/split_columns/pallas_call | solution.py:114
  177.4 2.2 copy-done.1
  179.6 2.6 split_columns.3
  182.3 6.8 %split_rows.7 = (bf16[8,512,512]{2,1,0:T(8,128)(2,1)S(1)}, bf16[8,512,512]{2,1,0:T(8,128)(2,1)S(1)}, f32[256,128]{1,0:T(8,128)S(1)}) custom-call(s32[17]{0:T(128)S(1)} %concatenate.25.facts_ref, f32[4,128,512]{2,1,0:T(8,128)S(1)} %pad_maximum_fusion.1.refs_0_, f32[4,128,512]{2,1,0:T(8,128)S(1)} %pad_maximum_fusion.2.refs_1_, f32[4,128,512]{2,1,0:T(8,128)S(1)} %copy-done.16, ...), custom_call_target="tpu_custom_call" | custom-call | flops 10485760 | bytes 12582912 | tf_op jit(solution)/shard_map/split_rows/pallas_call | solution.py:174
  189.1 1.9 copy-done.37
  191.1 2.0 copy-done.39
  193.8 6.2 %split_rows.6 = (bf16[8,512,512]{2,1,0:T(8,128)(2,1)S(1)}, bf16[8,512,512]{2,1,0:T(8,128)(2,1)S(1)}, f32[256,128]{1,0:T(8,128)S(1)}) custom-call(s32[17]{0:T(128)S(1)} %concatenate.25.facts_ref, f32[4,128,512]{2,1,0:T(8,128)} %collective-permute-done.17.refs_0_, f32[4,128,512]{2,1,0:T(8,128)} %collective-permute-done.23.refs_1_, ...), custom_call_target="tpu_custom_call" | custom-call | flops 10485760 | bytes 12582912 | tf_op jit(solution)/shard_map/split_rows/pallas_call | solution.py:174
  200.0 2.0 copy-done.41
  202.0 2.1 copy-done.43
  204.1 2.2 copy-done.38
  206.3 2.2 copy-done.40
  208.5 11.5 %product.4 = (f32[2,4,128,512]{3,2,1,0:T(8,128)}, f32[2,4,128,512]{3,2,1,0:T(8,128)}) custom-call(s32[9]{0:T(128)S(1)} %concatenate.28.facts_ref, bf16[8,512,512]{2,1,0:T(8,128)(2,1)S(1)} %copy-done.38, bf16[8,512,512]{2,1,0:T(8,128)(2,1)S(1)} %copy-done.40, f32[256,128]{1,0:T(8,128)S(1)} %get-tuple-element.127.edge, bf16[8,512,512]{2,1,0:T(8,128)(2,1)S(1)} %bitcast.52, ...), custom_call_target="tpu_custom_call" | custom-call | flops 6442450944 | bytes 16777216 | tf_op jit(solution)/shard_map/product/pallas_call | solution.py:230
  220.0 6.5 %split_rows.5 = (bf16[8,512,512]{2,1,0:T(8,128)(2,1)S(1)}, bf16[8,512,512]{2,1,0:T(8,128)(2,1)S(1)}, f32[256,128]{1,0:T(8,128)S(1)}) custom-call(s32[17]{0:T(128)S(1)} %concatenate.25.facts_ref, f32[4,128,512]{2,1,0:T(8,128)S(1)} %copy-done.12, f32[4,128,512]{2,1,0:T(8,128)} %collective-permute-done.24.refs_1_, ...), custom_call_target="tpu_custom_call" | custom-call | flops 10485760 | bytes 12582912 | tf_op jit(solution)/shard_map/split_rows/pallas_call | solution.py:174
  226.5 1.9 copy-done.45
  228.5 2.2 copy-done.44
  230.7 11.5 %product.5 = (f32[2,4,128,512]{3,2,1,0:T(8,128)}, f32[2,4,128,512]{3,2,1,0:T(8,128)}) custom-call(s32[9]{0:T(128)S(1)} %concatenate.27.facts_ref, bf16[8,512,512]{2,1,0:T(8,128)(2,1)S(1)} %copy-done.42, bf16[8,512,512]{2,1,0:T(8,128)(2,1)S(1)} %copy-done.44, f32[256,128]{1,0:T(8,128)S(1)} %get-tuple-element.122.edge, ...), custom_call_target="tpu_custom_call", output_to_operand_aliasing={{0}: (7, {}), {1}: (8, {})} | custom-call | flops 6442450944 | bytes 16777216 | tf_op jit(solution)/shard_map/product/pallas_call | solution.py:230
  242.1 2.2 copy-done.46
  244.3 11.5 %product.6 = (f32[2,4,128,512]{3,2,1,0:T(8,128)}, f32[2,4,128,512]{3,2,1,0:T(8,128)}) custom-call(s32[9]{0:T(128)S(1)} %concatenate.26.facts_ref, bf16[8,512,512]{2,1,0:T(8,128)(2,1)S(1)} %copy-done.46, bf16[8,512,512]{2,1,0:T(8,128)(2,1)S(1)} %get-tuple-element.117.al, ...), custom_call_target="tpu_custom_call", output_to_operand_aliasing={{0}: (7, {}), {1}: (8, {})} | custom-call | flops 6442450944 | bytes 16777216 | tf_op jit(solution)/shard_map/product/pallas_call | solution.py:230
  255.8 5.8 %split_rows.4 = (bf16[8,512,512]{2,1,0:T(8,128)(2,1)S(1)}, bf16[8,512,512]{2,1,0:T(8,128)(2,1)S(1)}, f32[256,128]{1,0:T(8,128)S(1)}) custom-call(s32[17]{0:T(128)S(1)} %concatenate.25.facts_ref, f32[4,128,512]{2,1,0:T(8,128)} %collective-permute-done.29.refs_0_, f32[4,128,512]{2,1,0:T(8,128)} %collective-permute-done.30.refs_1_, ...), custom_call_target="tpu_custom_call" | custom-call | flops 10485760 | bytes 12582912 | tf_op jit(solution)/shard_map/split_rows/pallas_call | solution.py:174
  261.7 11.5 %product.7 = (f32[2,4,128,512]{3,2,1,0:T(8,128)}, f32[2,4,128,512]{3,2,1,0:T(8,128)}) custom-call(s32[9]{0:T(128)S(1)} %concatenate.24.facts_ref, bf16[8,512,512]{2,1,0:T(8,128)(2,1)S(1)} %get-tuple-element.97.ah, bf16[8,512,512]{2,1,0:T(8,128)(2,1)S(1)} %get-tuple-element.98.al, ...), custom_call_target="tpu_custom_call", output_to_operand_aliasing={{0}: (7, {}), {1}: (8, {})} | custom-call | flops 6442450944 | bytes 16777216 | tf_op jit(solution)/shard_map/product/pallas_call | solution.py:230
  (148 shorter events, 29.2 us)
Async XLA Ops:
  2.6 50.3 %copy-start = (f32[512,512]{1,0:T(8,128)S(1)}, f32[512,512]{1,0:T(8,128)}, u32[]{:S(2)}) copy-start(f32[512,512]{1,0:T(8,128)} %refs_0_) | copy-start | bytes 3145732
  2.6 11.6 %collective-permute-start = (f32[128,512]{0,1:T(8,128)S(1)}, f32[128,512]{0,1:T(8,128)S(1)}, u32[]{:S(2)}, u32[]{:S(2)}) collective-permute-start(f32[128,512]{0,1:T(8,128)S(1)} %get-tuple-element.142), channel_id=1, source_target_pairs={{0,2},{1,3},{2,4},{3,5},{4,6},{5,7},{6,0},{7,1},{8,10},{9,11},{10,... | collective-permute-start | bytes 786440 | tf_op jit(solution)/shard_map/ppermute | solution.py:28
  7.0 18.3 %collective-permute-start.3 = (f32[256,512]{1,0:T(8,128)}, f32[256,512]{1,0:T(8,128)S(1)}, u32[]{:S(2)}, u32[]{:S(2)}) collective-permute-start(f32[256,512]{1,0:T(8,128)} %slice.44), channel_id=1, source_target_pairs={{0,32},{1,33},{2,34},{3,35},{4,36},{5,37},{6,38},{7,39},{8,40},{9,... | collective-permute-start | bytes 1572872 | tf_op jit(solution)/shard_map/ppermute | solution.py:28
  8.2 17.0 %collective-permute-start.4 = (f32[256,512]{1,0:T(8,128)}, f32[256,512]{1,0:T(8,128)S(1)}, u32[]{:S(2)}, u32[]{:S(2)}) collective-permute-start(f32[256,512]{1,0:T(8,128)} %slice.44), channel_id=1, source_target_pairs={{0,96},{1,97},{2,98},{3,99},{4,100},{5,101},{6,102},{7,103},{8,104... | collective-permute-start | bytes 1572872 | tf_op jit(solution)/shard_map/ppermute | solution.py:28
  9.7 15.6 %collective-permute-start.5 = (f32[256,512]{1,0:T(8,128)}, f32[256,512]{1,0:T(8,128)S(1)}, u32[]{:S(2)}, u32[]{:S(2)}) collective-permute-start(f32[256,512]{1,0:T(8,128)} %slice.44), channel_id=1, source_target_pairs={{0,16},{1,17},{2,18},{3,19},{4,20},{5,21},{6,22},{7,23},{8,24},{9,... | collective-permute-start | bytes 1572872 | tf_op jit(solution)/shard_map/ppermute | solution.py:28
  10.9 8.5 %collective-permute-start.1 = (f32[128,512]{0,1:T(8,128)}, f32[128,512]{0,1:T(8,128)}, u32[]{:S(2)}, u32[]{:S(2)}) collective-permute-start(f32[128,512]{0,1:T(8,128)} %get-tuple-element.141), channel_id=1, source_target_pairs={{0,4},{1,5},{2,6},{3,7},{4,0},{5,1},{6,2},{7,3},{8,12},{9,13},{10,... | collective-permute-start | bytes 786440 | tf_op jit(solution)/shard_map/ppermute | solution.py:28
  14.2 11.0 %collective-permute-start.2 = (f32[128,512]{0,1:T(8,128)S(1)}, f32[128,512]{0,1:T(8,128)}, u32[]{:S(2)}, u32[]{:S(2)}) collective-permute-start(f32[128,512]{0,1:T(8,128)S(1)} %get-tuple-element.140), channel_id=1, source_target_pairs={{0,6},{1,7},{2,0},{3,1},{4,2},{5,3},{6,4},{7,5},{8,14},{9,15},{10,... | collective-permute-start | bytes 786440 | tf_op jit(solution)/shard_map/ppermute | solution.py:28
  25.3 42.6 %copy-start.17 = (f32[256,512]{1,0:T(8,128)}, f32[256,512]{1,0:T(8,128)S(1)}, u32[]{:S(2)}) copy-start(f32[256,512]{1,0:T(8,128)S(1)} %collective-permute-done.3.refs_3_) | copy-start | bytes 1572868
  25.3 42.6 %copy-start.19 = (f32[256,512]{1,0:T(8,128)}, f32[256,512]{1,0:T(8,128)S(1)}, u32[]{:S(2)}) copy-start(f32[256,512]{1,0:T(8,128)S(1)} %collective-permute-done.4.refs_5_) | copy-start | bytes 1572868
  25.3 64.4 %copy-start.21 = (f32[256,512]{1,0:T(8,128)}, f32[256,512]{1,0:T(8,128)S(1)}, u32[]{:S(2)}) copy-start(f32[256,512]{1,0:T(8,128)S(1)} %collective-permute-done.5.refs_1_) | copy-start | bytes 1572868
  29.3 10.0 %collective-permute-start.6 = (f32[128,512]{1,0:T(8,128)}, f32[128,512]{1,0:T(8,128)}, u32[]{:S(2)}, u32[]{:S(2)}) collective-permute-start(f32[128,512]{1,0:T(8,128)} %bitcast.61), channel_id=1, source_target_pairs={{0,0},{1,1},{2,2},{3,3},{4,4},{5,5},{6,6},{7,7},{8,72},{9,73},{10,... | collective-permute-start | bytes 786440 | tf_op jit(solution)/shard_map/ppermute | solution.py:28
  33.8 6.4 %collective-permute-start.7 = (f32[128,512]{1,0:T(8,128)}, f32[128,512]{1,0:T(8,128)}, u32[]{:S(2)}, u32[]{:S(2)}) collective-permute-start(f32[128,512]{1,0:T(8,128)} %bitcast.62), channel_id=1, source_target_pairs={{0,16},{1,17},{2,18},{3,19},{4,20},{5,21},{6,22},{7,23},{8,88},{9,... | collective-permute-start | bytes 786440 | tf_op jit(solution)/shard_map/ppermute | solution.py:28
  34.4 13.7 %collective-permute-start.8 = (f32[128,512]{1,0:T(8,128)S(1)}, f32[128,512]{1,0:T(8,128)}, u32[]{:S(2)}, u32[]{:S(2)}) collective-permute-start(f32[128,512]{1,0:T(8,128)S(1)} %bitcast.63), channel_id=1, source_target_pairs={{0,40},{1,41},{2,42},{3,43},{4,44},{5,45},{6,46},{7,47},{8,96},{9,... | collective-permute-start | bytes 786440 | tf_op jit(solution)/shard_map/ppermute | solution.py:28
  38.4 14.5 %collective-permute-start.9 = (f32[128,512]{1,0:T(8,128)S(1)}, f32[128,512]{1,0:T(8,128)S(1)}, u32[]{:S(2)}, u32[]{:S(2)}) collective-permute-start(f32[128,512]{1,0:T(8,128)S(1)} %bitcast.64), channel_id=1, source_target_pairs={{0,56},{1,57},{2,58},{3,59},{4,60},{5,61},{6,62},{7,63},{8,112},{9... | collective-permute-start | bytes 786440 | tf_op jit(solution)/shard_map/ppermute | solution.py:28
  53.0 14.8 %collective-permute-start.12 = (f32[256,512]{1,0:T(8,128)S(1)}, f32[256,512]{1,0:T(8,128)S(1)}, u32[]{:S(2)}, u32[]{:S(2)}) collective-permute-start(f32[256,512]{1,0:T(8,128)S(1)} %slice.45), channel_id=1, source_target_pairs={{0,32},{1,33},{2,34},{3,35},{4,36},{5,37},{6,38},{7,39},{8,40},{9,... | collective-permute-start | bytes 1572872 | tf_op jit(solution)/shard_map/ppermute | solution.py:28
  53.0 14.8 %collective-permute-start.13 = (f32[256,512]{1,0:T(8,128)S(1)}, f32[256,512]{1,0:T(8,128)S(1)}, u32[]{:S(2)}, u32[]{:S(2)}) collective-permute-start(f32[256,512]{1,0:T(8,128)S(1)} %slice.45), channel_id=1, source_target_pairs={{0,96},{1,97},{2,98},{3,99},{4,100},{5,101},{6,102},{7,103},{8,104... | collective-permute-start | bytes 1572872 | tf_op jit(solution)/shard_map/ppermute | solution.py:28
  55.7 6.9 %collective-permute-start.10 = (f32[128,512]{1,0:T(8,128)}, f32[128,512]{1,0:T(8,128)S(1)}, u32[]{:S(2)}, u32[]{:S(2)}) collective-permute-start(f32[128,512]{1,0:T(8,128)} %collective-permute-done.6), channel_id=1, source_target_pairs={{0,8},{1,9},{2,10},{3,11},{4,12},{5,13},{6,14},{7,15},{8,0},{9,1},... | collective-permute-start | bytes 786440 | tf_op jit(solution)/shard_map/ppermute | solution.py:28
  56.7 11.1 %collective-permute-start.11 = (f32[128,512]{1,0:T(8,128)}, f32[128,512]{1,0:T(8,128)S(1)}, u32[]{:S(2)}, u32[]{:S(2)}) collective-permute-start(f32[128,512]{1,0:T(8,128)} %collective-permute-done.7), channel_id=1, source_target_pairs={{0,8},{1,9},{2,10},{3,11},{4,12},{5,13},{6,14},{7,15},{8,0},{9,1},... | collective-permute-start | bytes 786440 | tf_op jit(solution)/shard_map/ppermute | solution.py:28
  58.7 17.8 %collective-permute-start.19 = (f32[256,512]{1,0:T(8,128)S(1)}, f32[256,512]{1,0:T(8,128)S(1)}, u32[]{:S(2)}, u32[]{:S(2)}) collective-permute-start(f32[256,512]{1,0:T(8,128)S(1)} %collective-permute-done.3.refs_3_), channel_id=1, source_target_pairs={{0,32},{1,33},{2,34},{3,35},{4,36},{5,37},{6,38},{7,39},{8,40},{9,... | collective-permute-start | bytes 1572872 | tf_op jit(solution)/shard_map/ppermute | solution.py:28
  67.8 83.3 %copy-start.25 = (f32[256,512]{1,0:T(8,128)}, f32[256,512]{1,0:T(8,128)S(1)}, u32[]{:S(2)}) copy-start(f32[256,512]{1,0:T(8,128)S(1)} %collective-permute-done.13.refs_6_) | copy-start | bytes 1572868
  67.9 21.8 %collective-permute-start.16 = (f32[256,512]{1,0:T(8,128)S(1)}, f32[256,512]{1,0:T(8,128)S(1)}, u32[]{:S(2)}, u32[]{:S(2)}) collective-permute-start(f32[256,512]{1,0:T(8,128)S(1)} %slice.46), channel_id=1, source_target_pairs={{0,16},{1,17},{2,18},{3,19},{4,20},{5,21},{6,22},{7,23},{8,24},{9,... | collective-permute-start | bytes 1572872 | tf_op jit(solution)/shard_map/ppermute | solution.py:28
  69.7 34.9 %collective-permute-start.17 = (f32[4,128,512]{2,1,0:T(8,128)S(1)}, f32[4,128,512]{2,1,0:T(8,128)}, u32[]{:S(2)}, u32[]{:S(2)}) collective-permute-start(f32[4,128,512]{2,1,0:T(8,128)S(1)} %pad_maximum_fusion.1.refs_0_), channel_id=1, source_target_pairs={{0,2},{1,3},{2,4},{3,5},{4,6},{5,7},{6,0},{7,1},{8,10},{9,11},{10,... | collective-permute-start | bytes 3145736 | tf_op jit(solution)/shard_map/ppermute | solution.py:28
  73.9 30.7 %collective-permute-start.18 = (f32[4,128,512]{2,1,0:T(8,128)S(1)}, f32[4,128,512]{2,1,0:T(8,128)S(1)}, u32[]{:S(2)}, u32[]{:S(2)}) collective-permute-start(f32[4,128,512]{2,1,0:T(8,128)S(1)} %pad_maximum_fusion.1.refs_0_), channel_id=1, source_target_pairs={{0,6},{1,7},{2,0},{3,1},{4,2},{5,3},{6,4},{7,5},{8,14},{9,15},{10,... | collective-permute-start | bytes 3145736 | tf_op jit(solution)/shard_map/ppermute | solution.py:28
  73.9 9.8 %collective-permute-start.14 = (f32[128,512]{1,0:T(8,128)}, f32[128,512]{1,0:T(8,128)S(1)}, u32[]{:S(2)}, u32[]{:S(2)}) collective-permute-start(f32[128,512]{1,0:T(8,128)} %collective-permute-done.8), channel_id=1, source_target_pairs={{0,8},{1,9},{2,10},{3,11},{4,12},{5,13},{6,14},{7,15},{8,0},{9,1},... | collective-permute-start | bytes 786440 | tf_op jit(solution)/shard_map/ppermute | solution.py:28
  77.3 12.3 %collective-permute-start.15 = (f32[128,512]{1,0:T(8,128)S(1)}, f32[128,512]{1,0:T(8,128)S(1)}, u32[]{:S(2)}, u32[]{:S(2)}) collective-permute-start(f32[128,512]{1,0:T(8,128)S(1)} %collective-permute-done.9), channel_id=1, source_target_pairs={{0,8},{1,9},{2,10},{3,11},{4,12},{5,13},{6,14},{7,15},{8,0},{9,1},... | collective-permute-start | bytes 786440 | tf_op jit(solution)/shard_map/ppermute | solution.py:28
  83.7 8.6 %collective-permute-start.20 = (f32[256,512]{1,0:T(8,128)S(1)}, f32[256,512]{1,0:T(8,128)S(1)}, u32[]{:S(2)}, u32[]{:S(2)}) collective-permute-start(f32[256,512]{1,0:T(8,128)S(1)} %collective-permute-done.13.refs_6_), channel_id=1, source_target_pairs={{0,96},{1,97},{2,98},{3,99},{4,100},{5,101},{6,102},{7,103},{8,104... | collective-permute-start | bytes 1572872 | tf_op jit(solution)/shard_map/ppermute | solution.py:28
  89.6 10.0 %collective-permute-start.21 = (f32[256,512]{1,0:T(8,128)S(1)}, f32[256,512]{1,0:T(8,128)S(1)}, u32[]{:S(2)}, u32[]{:S(2)}) collective-permute-start(f32[256,512]{1,0:T(8,128)S(1)} %collective-permute-done.5.refs_1_), channel_id=1, source_target_pairs={{0,32},{1,33},{2,34},{3,35},{4,36},{5,37},{6,38},{7,39},{8,40},{9,... | collective-permute-start | bytes 1572872 | tf_op jit(solution)/shard_map/ppermute | solution.py:28
  89.7 14.9 %collective-permute-start.22 = (f32[256,512]{1,0:T(8,128)S(1)}, f32[256,512]{1,0:T(8,128)S(1)}, u32[]{:S(2)}, u32[]{:S(2)}) collective-permute-start(f32[256,512]{1,0:T(8,128)S(1)} %collective-permute-done.5.refs_1_), channel_id=1, source_target_pairs={{0,96},{1,97},{2,98},{3,99},{4,100},{5,101},{6,102},{7,103},{8,104... | collective-permute-start | bytes 1572872 | tf_op jit(solution)/shard_map/ppermute | solution.py:28
  99.6 49.4 %copy-start.7 = (f32[256,512]{1,0:T(8,128)}, f32[256,512]{1,0:T(8,128)S(1)}, u32[]{:S(2)}) copy-start(f32[256,512]{1,0:T(8,128)S(1)} %collective-permute-done.21.refs_9_) | copy-start | bytes 1572868
  104.6 46.5 %copy-start.9 = (f32[256,512]{1,0:T(8,128)}, f32[256,512]{1,0:T(8,128)S(1)}, u32[]{:S(2)}) copy-start(f32[256,512]{1,0:T(8,128)S(1)} %collective-permute-done.22.refs_10_) | copy-start | bytes 1572868
  106.7 28.0 %collective-permute-start.23 = (f32[4,128,512]{2,1,0:T(8,128)S(1)}, f32[4,128,512]{2,1,0:T(8,128)}, u32[]{:S(2)}, u32[]{:S(2)}) collective-permute-start(f32[4,128,512]{2,1,0:T(8,128)S(1)} %pad_maximum_fusion.2.refs_1_), channel_id=1, source_target_pairs={{0,2},{1,3},{2,4},{3,5},{4,6},{5,7},{6,0},{7,1},{8,10},{9,11},{10,... | collective-permute-start | bytes 3145736 | tf_op jit(solution)/shard_map/ppermute | solution.py:28
  111.2 23.5 %collective-permute-start.24 = (f32[4,128,512]{2,1,0:T(8,128)S(1)}, f32[4,128,512]{2,1,0:T(8,128)}, u32[]{:S(2)}, u32[]{:S(2)}) collective-permute-start(f32[4,128,512]{2,1,0:T(8,128)S(1)} %pad_maximum_fusion.2.refs_1_), channel_id=1, source_target_pairs={{0,6},{1,7},{2,0},{3,1},{4,2},{5,3},{6,4},{7,5},{8,14},{9,15},{10,... | collective-permute-start | bytes 3145736 | tf_op jit(solution)/shard_map/ppermute | solution.py:28
  111.2 23.4 %collective-permute-start.25 = (f32[256,512]{1,0:T(8,128)S(1)}, f32[256,512]{1,0:T(8,128)S(1)}, u32[]{:S(2)}, u32[]{:S(2)}) collective-permute-start(f32[256,512]{1,0:T(8,128)S(1)} %collective-permute-done.16.refs_2_), channel_id=1, source_target_pairs={{0,32},{1,33},{2,34},{3,35},{4,36},{5,37},{6,38},{7,39},{8,40},{9,... | collective-permute-start | bytes 1572872 | tf_op jit(solution)/shard_map/ppermute | solution.py:28
  113.3 11.4 %collective-permute-start.27 = (f32[128,512]{1,0:T(8,128)S(1)}, f32[128,512]{1,0:T(8,128)S(1)}, u32[]{:S(2)}, u32[]{:S(2)}) collective-permute-start(f32[128,512]{1,0:T(8,128)S(1)} %slice.47), channel_id=1, source_target_pairs={{0,32},{1,33},{2,34},{3,35},{4,36},{5,37},{6,38},{7,39},{8,40},{9,... | collective-permute-start | bytes 786440 | tf_op jit(solution)/shard_map/ppermute | solution.py:28
  113.5 12.6 %collective-permute-start.28 = (f32[128,512]{1,0:T(8,128)S(1)}, f32[128,512]{1,0:T(8,128)S(1)}, u32[]{:S(2)}, u32[]{:S(2)}) collective-permute-start(f32[128,512]{1,0:T(8,128)S(1)} %slice.48), channel_id=1, source_target_pairs={{0,96},{1,97},{2,98},{3,99},{4,100},{5,101},{6,102},{7,103},{8,104... | collective-permute-start | bytes 786440 | tf_op jit(solution)/shard_map/ppermute | solution.py:28
  124.7 10.0 %collective-permute-start.26 = (f32[256,512]{1,0:T(8,128)S(1)}, f32[256,512]{1,0:T(8,128)S(1)}, u32[]{:S(2)}, u32[]{:S(2)}) collective-permute-start(f32[256,512]{1,0:T(8,128)S(1)} %collective-permute-done.16.refs_2_), channel_id=1, source_target_pairs={{0,96},{1,97},{2,98},{3,99},{4,100},{5,101},{6,102},{7,103},{8,104... | collective-permute-start | bytes 1572872 | tf_op jit(solution)/shard_map/ppermute | solution.py:28
  126.8 17.4 %collective-permute-start.39 = (f32[4,128,512]{2,1,0:T(8,128)S(1)}, f32[4,128,512]{2,1,0:T(8,128)S(1)}, u32[]{:S(2)}, u32[]{:S(2)}) collective-permute-start(f32[4,128,512]{2,1,0:T(8,128)S(1)} %pad_maximum_fusion.1.refs_0_), channel_id=1, source_target_pairs={{0,1},{1,0},{2,3},{3,2},{4,5},{5,4},{6,7},{7,6},{8,9},{9,8},{10,11... | collective-permute-start | bytes 3145736 | tf_op jit(solution)/shard_map/ppermute | solution.py:28
  134.6 9.6 %copy-start.3 = (f32[256,512]{1,0:T(8,128)}, f32[256,512]{1,0:T(8,128)S(1)}, u32[]{:S(2)}) copy-start(f32[256,512]{1,0:T(8,128)S(1)} %collective-permute-done.25.refs_0_) | copy-start | bytes 1572868
  134.6 11.8 %collective-permute-start.37 = (f32[4,128,512]{2,1,0:T(8,128)}, f32[4,128,512]{2,1,0:T(8,128)S(1)}, u32[]{:S(2)}, u32[]{:S(2)}) collective-permute-start(f32[4,128,512]{2,1,0:T(8,128)} %collective-permute-done.17.refs_0_), channel_id=1, source_target_pairs={{0,1},{1,0},{2,3},{3,2},{4,5},{5,4},{6,7},{7,6},{8,9},{9,8},{10,11... | collective-permute-start | bytes 3145736 | tf_op jit(solution)/shard_map/ppermute | solution.py:28
  134.7 26.1 %collective-permute-start.40 = (f32[4,128,512]{2,1,0:T(8,128)S(1)}, f32[4,128,512]{2,1,0:T(8,128)}, u32[]{:S(2)}, u32[]{:S(2)}) collective-permute-start(f32[4,128,512]{2,1,0:T(8,128)S(1)} %pad_maximum_fusion.2.refs_1_), channel_id=1, source_target_pairs={{0,1},{1,0},{2,3},{3,2},{4,5},{5,4},{6,7},{7,6},{8,9},{9,8},{10,11... | collective-permute-start | bytes 3145736 | tf_op jit(solution)/shard_map/ppermute | solution.py:28
  141.6 9.5 %collective-permute-start.33 = (f32[128,512]{1,0:T(8,128)S(1)}, f32[128,512]{1,0:T(8,128)S(1)}, u32[]{:S(2)}, u32[]{:S(2)}) collective-permute-start(f32[128,512]{1,0:T(8,128)S(1)} %slice.49), channel_id=1, source_target_pairs={{0,32},{1,33},{2,34},{3,35},{4,36},{5,37},{6,38},{7,39},{8,40},{9,... | collective-permute-start | bytes 786440 | tf_op jit(solution)/shard_map/ppermute | solution.py:28
  142.7 50.4 %collective-permute-start.29 = (f32[4,128,512]{2,1,0:T(8,128)}, f32[4,128,512]{2,1,0:T(8,128)}, u32[]{:S(2)}, u32[]{:S(2)}) collective-permute-start(f32[4,128,512]{2,1,0:T(8,128)} %collective-permute-done.17.refs_0_), channel_id=1, source_target_pairs={{0,2},{1,3},{2,4},{3,5},{4,6},{5,7},{6,0},{7,1},{8,10},{9,11},{10,... | collective-permute-start | bytes 3145736 | tf_op jit(solution)/shard_map/ppermute | solution.py:28
  145.2 48.3 %collective-permute-start.30 = (f32[4,128,512]{2,1,0:T(8,128)}, f32[4,128,512]{2,1,0:T(8,128)}, u32[]{:S(2)}, u32[]{:S(2)}) collective-permute-start(f32[4,128,512]{2,1,0:T(8,128)} %collective-permute-done.24.refs_1_), channel_id=1, source_target_pairs={{0,6},{1,7},{2,0},{3,1},{4,2},{5,3},{6,4},{7,5},{8,14},{9,15},{10,... | collective-permute-start | bytes 3145736 | tf_op jit(solution)/shard_map/ppermute | solution.py:28
  147.4 46.4 %collective-permute-start.38 = (f32[4,128,512]{2,1,0:T(8,128)}, f32[4,128,512]{2,1,0:T(8,128)}, u32[]{:S(2)}, u32[]{:S(2)}) collective-permute-start(f32[4,128,512]{2,1,0:T(8,128)} %collective-permute-done.23.refs_1_), channel_id=1, source_target_pairs={{0,1},{1,0},{2,3},{3,2},{4,5},{5,4},{6,7},{7,6},{8,9},{9,8},{10,11... | collective-permute-start | bytes 3145736 | tf_op jit(solution)/shard_map/ppermute | solution.py:28
  151.8 7.5 %collective-permute-start.34 = (f32[128,512]{1,0:T(8,128)}, f32[128,512]{1,0:T(8,128)}, u32[]{:S(2)}, u32[]{:S(2)}) collective-permute-start(f32[128,512]{1,0:T(8,128)} %slice.50), channel_id=1, source_target_pairs={{0,96},{1,97},{2,98},{3,99},{4,100},{5,101},{6,102},{7,103},{8,104... | collective-permute-start | bytes 786440 | tf_op jit(solution)/shard_map/ppermute | solution.py:28
  159.3 60.7 %collective-permute-start.35 = (f32[4,128,512]{2,1,0:T(8,128)}, f32[4,128,512]{2,1,0:T(8,128)}, u32[]{:S(2)}, u32[]{:S(2)}) collective-permute-start(f32[4,128,512]{2,1,0:T(8,128)} %copy-done.11), channel_id=1, source_target_pairs={{0,1},{1,0},{2,3},{3,2},{4,5},{5,4},{6,7},{7,6},{8,9},{9,8},{10,11... | collective-permute-start | bytes 3145736 | tf_op jit(solution)/shard_map/ppermute | solution.py:28
  160.9 59.2 %collective-permute-start.36 = (f32[4,128,512]{2,1,0:T(8,128)}, f32[4,128,512]{2,1,0:T(8,128)}, u32[]{:S(2)}, u32[]{:S(2)}) collective-permute-start(f32[4,128,512]{2,1,0:T(8,128)} %collective-permute-done.24.refs_1_), channel_id=1, source_target_pairs={{0,1},{1,0},{2,3},{3,2},{4,5},{5,4},{6,7},{7,6},{8,9},{9,8},{10,11... | collective-permute-start | bytes 3145736 | tf_op jit(solution)/shard_map/ppermute | solution.py:28
  162.3 15.1 %copy-start.4 = (f32[256,512]{1,0:T(8,128)S(1)}, f32[256,512]{1,0:T(8,128)}, u32[]{:S(2)}) copy-start(f32[256,512]{1,0:T(8,128)} %copy-done.3) | copy-start | bytes 1572868
  162.3 15.1 %copy-start.6 = (f32[256,512]{1,0:T(8,128)S(1)}, f32[256,512]{1,0:T(8,128)}, u32[]{:S(2)}) copy-start(f32[256,512]{1,0:T(8,128)} %copy-done.5) | copy-start | bytes 1572868
  173.8 3.6 %copy-start.36 = (f32[128,512]{1,0:T(8,128)S(1)}, f32[128,512]{1,0:T(8,128)}, u32[]{:S(2)}) copy-start(f32[128,512]{1,0:T(8,128)} %copy-done.35) | copy-start | bytes 786436
  177.4 2.2 copy-start.1
  179.6 2.7 copy-start.16
  182.3 17.7 %copy-start.2 = (bf16[4096,512]{1,0:T(8,128)(2,1)}, bf16[4096,512]{1,0:T(8,128)(2,1)S(1)}, u32[]{:S(2)}) copy-start(bf16[4096,512]{1,0:T(8,128)(2,1)S(1)} %get-tuple-element.113) | copy-start | bytes 12582916
  182.3 11.5 %copy-start.14 = (f32[4,128,512]{2,1,0:T(8,128)S(1)}, f32[4,128,512]{2,1,0:T(8,128)}, u32[]{:S(2)}) copy-start(f32[4,128,512]{2,1,0:T(8,128)} %copy-done.13) | copy-start | bytes 3145732
  193.1 62.7 %collective-permute-start.31 = (f32[4,128,512]{2,1,0:T(8,128)}, f32[4,128,512]{2,1,0:T(8,128)S(1)}, u32[]{:S(2)}, u32[]{:S(2)}) collective-permute-start(f32[4,128,512]{2,1,0:T(8,128)} %collective-permute-done.29.refs_0_), channel_id=1, source_target_pairs={{0,1},{1,0},{2,3},{3,2},{4,5},{5,4},{6,7},{7,6},{8,9},{9,8},{10,11... | collective-permute-start | bytes 3145736 | tf_op jit(solution)/shard_map/ppermute | solution.py:28
  193.5 62.3 %collective-permute-start.32 = (f32[4,128,512]{2,1,0:T(8,128)}, f32[4,128,512]{2,1,0:T(8,128)S(1)}, u32[]{:S(2)}, u32[]{:S(2)}) collective-permute-start(f32[4,128,512]{2,1,0:T(8,128)} %collective-permute-done.30.refs_1_), channel_id=1, source_target_pairs={{0,1},{1,0},{2,3},{3,2},{4,5},{5,4},{6,7},{7,6},{8,9},{9,8},{10,11... | collective-permute-start | bytes 3145736 | tf_op jit(solution)/shard_map/ppermute | solution.py:28
  200.0 2.0 copy-start.41
  202.0 2.1 copy-start.43
  204.1 2.2 copy-start.38
  206.3 2.2 copy-start.40
  208.5 11.5 %copy-start.12 = (f32[4,128,512]{2,1,0:T(8,128)S(1)}, f32[4,128,512]{2,1,0:T(8,128)}, u32[]{:S(2)}) copy-start(f32[4,128,512]{2,1,0:T(8,128)} %copy-done.11) | copy-start | bytes 3145732
  220.0 8.4 %copy-start.42 = (bf16[8,512,512]{2,1,0:T(8,128)(2,1)S(1)}, bf16[8,512,512]{2,1,0:T(8,128)(2,1)}, u32[]{:S(2)}) copy-start(bf16[8,512,512]{2,1,0:T(8,128)(2,1)} %copy-done.41) | copy-start | bytes 12582916
  228.5 2.2 copy-start.44
  242.1 2.2 copy-start.46
  (24 other events, 25.8 us)
